TPU v7x, 128 devices: a whole 4x4x4 slice. The times are simulated.
128 devices in a mesh: gx: 8 (over x, core), gy: 16 (over z, y).
Axes of the slice: x: 4, y: 4, z: 4, core: 2. Of those that a mesh axis runs over, the one named last changes fastest.
Arguments:
- equation_misfit: float32 [3, 16, 512, 2048], P(None, None, 'gx', 'gy'), may hold values from -6 to 6
- thermal_excess: float32 [16, 512, 2048], P(None, 'gx', 'gy'), may hold values from 0.5 to 1.5
- spanning_vectors: bfloat16 [8, 3, 16, 512, 2048], P(None, None, None, 'gx', 'gy'), may hold values from -6 to 6
- global_solve_pieces: float32 [32, 16, 9, 8, 8], P('gx', 'gy'), may hold values from -0.0009765625 to 0.0009765625
- influencing_partition_table: int32 [32, 16, 9], P('gx', 'gy'), may hold values from 0 to 511, as said below
- spanning_vector_tally: int32 [32, 16], P('gx', 'gy'), may hold values from 1 to 8
Outputs:
- preconditioned: float32 [3, 16, 512, 2048], P(None, None, 'gx', 'gy')
Inputs may be any that keep to these rules, and one draw needn't show every extreme that they name: `influencing_partition_table`: entries are subdomain numbers i * 16 + j.
All inputs are finite; a program needn't handle non-finite values.
Results may differ from a plain program's by a relative error of at most 0.0065.
Values sent between devices are 32-bit elements; how exact they have to be, the bound alone decides.
A program may use at most 192 MiB of HBM per device.

v0:
```python
import jax
import jax.numpy as jnp
from jax import lax
from jax.experimental import pallas as pl
from jax.experimental.pallas import tpu as pltpu
from jax.sharding import PartitionSpec as P

F32 = jnp.float32
BF16 = jnp.bfloat16
MESH = pl.DeviceIdType.MESH

COMPS = 3
DEPTH = 16
ROWS = 64
LANES = 128
SUBS = 4
SX = 16
KMAX = 8
NLIST = 9

MASS_TERM = 0.05
RELAX_WEIGHT = 0.8
ARRHENIUS_FACTOR = 6.0


def kernel(
    b_hbm,
    te_hbm,
    v_hbm,
    g_ref,
    table_ref,
    tally_ref,
    out_hbm,
    te_t,
    b_t,
    b_n,
    v_n,
    shear,
    shear_lr,
    edge_own,
    edge_got,
    rows_own,
    rows_got,
    corner_got,
    edge_m,
    edge_x,
    shift,
    x0,
    x1,
    lhs0,
    lhs1,
    lr0,
    lr1,
    s0,
    s1,
    gl,
    gr,
    xr0,
    xr1,
    lhsr0,
    lhsr1,
    lrr0,
    lrr1,
    sr0,
    sr1,
    loc_t,
    loc_n,
    gx_pieces,
    coarse,
    sol,
    te_sem,
    bt_sem,
    bn_sem,
    v_sem,
    loc_sem,
    out_sem,
    halo_send,
    halo_recv,
    one_send,
    one_recv,
    two_send,
    two_recv,
):
    gx = lax.axis_index("gx")
    gy = lax.axis_index("gy")
    nx = lax.axis_size("gx")
    ny = lax.axis_size("gy")
    up, down = lax.rem(gx + nx - 1, nx), lax.rem(gx + 1, nx)
    left, right = lax.rem(gy + ny - 1, ny), lax.rem(gy + 1, ny)

    barrier = pltpu.get_barrier_semaphore()
    for o in range(1, nx):
        pl.semaphore_signal(barrier, 1, device_id=(lax.rem(gx + o, nx), gy), device_id_type=MESH)
    for o in range(1, ny):
        pl.semaphore_signal(barrier, 1, device_id=(gx, lax.rem(gy + o, ny)), device_id_type=MESH)
    for px in (up, down):
        for py in (left, right):
            pl.semaphore_signal(barrier, 1, device_id=(px, py), device_id_type=MESH)

    for d in range(DEPTH):
        pltpu.make_async_copy(te_hbm.at[d], te_t.at[:, d, :], te_sem).start()
    for c in range(COMPS):
        for d in range(DEPTH):
            pltpu.make_async_copy(b_hbm.at[c, d], b_t.at[c, :, d, :], bt_sem).start()
    pltpu.make_async_copy(b_hbm, b_n, bn_sem).start()
    half = DEPTH // 2

    def v_copy(c, h):
        part = pl.ds(h * half, half)
        return pltpu.make_async_copy(
            v_hbm.at[:, c, part], v_n.at[:, c, part], v_sem.at[c * 2 + h]
        )

    for c in range(COMPS):
        for h in range(2):
            v_copy(c, h).start()

    lane = lax.broadcasted_iota(jnp.int32, (DEPTH, LANES), 1)
    sub = lax.broadcasted_iota(jnp.int32, (DEPTH, LANES), 0)

    wi = lax.broadcasted_iota(jnp.int32, (2 * LANES, 2 * LANES), 0)
    wj = lax.broadcasted_iota(jnp.int32, (2 * LANES, 2 * LANES), 1)
    own, to_left = wi < LANES, wj < LANES
    hit = (
        (own & to_left & (wi == wj - 1))
        | (own & ~to_left & (wi == wj - LANES + 1))
        | (~own & ((wi & 3) == 3) & (wj == 0))
        | (~own & ((wi & 3) == 0) & (wj == 2 * LANES - 1))
    )
    shift[...] = jnp.where(hit, 1.0, 0.0).astype(BF16)

    ei = lax.broadcasted_iota(jnp.int32, (KMAX, LANES), 0)
    ej = lax.broadcasted_iota(jnp.int32, (KMAX, LANES), 1)
    spread = jnp.where(((ej & (KMAX - 1)) == ei) & (ej < SUBS * KMAX), 1.0, 0.0)
    gx_pieces[...] = jnp.dot(
        g_ref[...].reshape(SUBS * NLIST * KMAX, KMAX),
        spread,
        precision=lax.Precision.HIGHEST,
        preferred_element_type=F32,
    )

    zeros = jnp.zeros((COMPS, 8, LANES), F32)

    def clear(p, _):
        for ref in (x0, x1):
            ref[:, p, 0:8, :] = zeros
            ref[:, p, 24:32, :] = zeros
        return 0

    lax.fori_loop(0, ROWS + 2, clear, 0)

    def clear_cut(p, _):
        for ref in (xr0, xr1):
            ref[:, p, 0:8, :] = zeros
            ref[:, p, 24:32, :] = zeros
        return 0

    lax.fori_loop(0, 2 * SUBS, clear_cut, 0)

    def put_shear(p, m):
        shear[p, 8:24, :] = m
        shear[p, 7:8, :] = m[0:1]
        shear[p, 24:25, :] = m[15:16]

    pltpu.make_async_copy(te_t, te_t, te_sem).wait()

    def make_shear(i, _):
        for j in range(4):
            r = i * 4 + j
            m = 1.0 / (1.0 + jnp.exp(ARRHENIUS_FACTOR * (1.0 - 1.0 / te_t[r])))
            put_shear(r + 2, m)
        return 0

    lax.fori_loop(0, ROWS // 4, make_shear, 0)
    pltpu.make_async_copy(b_t, b_t, bt_sem).wait()

    slot = ((lane + 2) & (LANES - 1)) >> 2

    def pack(i, held):
        for j in range(2):
            rr = i * 2 + j
            here = slot == rr
            new = []
            for f in range(4):
                for h in range(2):
                    r = rr + 32 * h
                    val = shear[r + 2, 8:24, :] if f == 0 else b_t[f - 1, r]
                    new.append(jnp.where(here, pltpu.roll(val, 4 * rr, 1), held[f * 2 + h]))
            held = tuple(new)
        return held

    packed = lax.fori_loop(0, 16, pack, tuple(jnp.zeros((DEPTH, LANES), F32) for _ in range(8)))
    for i in range(8):
        edge_own[i] = packed[i]
    for side, (near, next_) in enumerate(((0, 1), (ROWS - 1, ROWS - 2))):
        rows_own[side, 0] = shear[near + 2, 8:24, :]
        rows_own[side, 1] = shear[next_ + 2, 8:24, :]
        for c in range(COMPS):
            rows_own[side, 2 + c] = b_t[c, near]

    pl.semaphore_wait(barrier, (nx - 1) + (ny - 1) + 4)

    def halo(i, src, dst, px, py):
        return pltpu.make_async_remote_copy(
            src_ref=src,
            dst_ref=dst,
            send_sem=halo_send.at[i],
            recv_sem=halo_recv.at[i],
            device_id=(px, py),
            device_id_type=MESH,
        )

    halos = [
        halo(0, rows_own.at[0], rows_got.at[1], up, gy),
        halo(1, rows_own.at[1], rows_got.at[0], down, gy),
        halo(2, edge_own, edge_got.at[1], gx, left),
        halo(3, edge_own, edge_got.at[0], gx, right),
        halo(4, rows_own.at[0, 0], corner_got.at[3], up, left),
        halo(5, rows_own.at[0, 0], corner_got.at[2], up, right),
        halo(6, rows_own.at[1, 0], corner_got.at[1], down, left),
        halo(7, rows_own.at[1, 0], corner_got.at[0], down, right),
    ]
    for copy in halos:
        copy.start()

    pltpu.make_async_copy(b_n, b_n, bn_sem).wait()
    accs = tuple(jnp.zeros((8, LANES), F32) for _ in range(SUBS * KMAX))
    for c in range(COMPS):
        for h in range(2):
            v_copy(c, h).wait()

            def restrict(d, accs):
                new = []
                for s in range(SUBS):
                    part = slice(s * SX, s * SX + SX)
                    low = b_n[c, d, part, :].astype(BF16).astype(F32)
                    for k in range(KMAX):
                        prod = v_n[k, c, d, part, :].astype(F32) * low
                        new.append(accs[s * KMAX + k] + (prod[:8] + prod[8:]))
                return tuple(new)

            accs = lax.fori_loop(h * half, h * half + half, restrict, accs)
    sums = jnp.stack(accs).sum(axis=1)
    totals = jnp.sum(sums, axis=1, keepdims=True)
    ri = lax.broadcasted_iota(jnp.int32, (SUBS * KMAX, LANES), 0)
    rj = lax.broadcasted_iota(jnp.int32, (SUBS * KMAX, LANES), 1)
    rhs = jnp.sum(jnp.where(ri == rj, totals, 0.0), axis=0, keepdims=True)
    lane1 = lax.broadcasted_iota(jnp.int32, (1, LANES), 1)
    limit = jnp.zeros((1, LANES), jnp.int32)
    for s in range(SUBS):
        limit = jnp.where((lane1 >> 3) == s, tally_ref[s, 0], limit)
    rhs = jnp.where((lane1 & (KMAX - 1)) < limit, rhs, 0.0)
    coarse[gy * nx + gx] = rhs

    def one(o, who):
        slot_ref = coarse.at[gy * nx + who]
        return pltpu.make_async_remote_copy(
            src_ref=slot_ref,
            dst_ref=slot_ref,
            send_sem=one_send.at[o - 1],
            recv_sem=one_recv.at[o - 1],
            device_id=(lax.rem(gx + o, nx), gy),
            device_id_type=MESH,
        )

    def two(o, who):
        slot_ref = coarse.at[pl.ds(who * nx, nx)]
        return pltpu.make_async_remote_copy(
            src_ref=slot_ref,
            dst_ref=slot_ref,
            send_sem=two_send.at[o - 1],
            recv_sem=two_recv.at[o - 1],
            device_id=(gx, lax.rem(gy + o, ny)),
            device_id_type=MESH,
        )

    for o in range(1, nx):
        one(o, gx).start()

    for copy in halos:
        copy.wait()

    def flag(cond):
        return jnp.where(cond, 1.0, 0.0).astype(F32)

    k_up, k_down = flag(gx > 0), flag(gx < nx - 1)
    k_left, k_right = flag(gy > 0), flag(gy < ny - 1)
    put_shear(1, rows_got[0, 0] * k_up)
    put_shear(0, rows_got[0, 1] * k_up)
    put_shear(ROWS + 2, rows_got[1, 0] * k_down)
    put_shear(ROWS + 3, rows_got[1, 1] * k_down)
    from_left = (lane & 3) >= 2
    got = [
        jnp.where(from_left, edge_got[0, i] * k_left, edge_got[1, i] * k_right) for i in range(8)
    ]
    corner_up = jnp.where(lane == LANES - 1, corner_got[0] * (k_up * k_left), corner_got[1] * (k_up * k_right))
    corner_down = jnp.where(lane == LANES - 1, corner_got[2] * (k_down * k_left), corner_got[3] * (k_down * k_right))
    first, last = slot == 0, slot == 31
    back4 = LANES - 4
    ups = [
        jnp.where(first, corner_up, pltpu.roll(got[0], 4, 1)),
        jnp.where(first, pltpu.roll(got[0], 4, 1), pltpu.roll(got[1], 4, 1)),
    ]
    downs = [
        jnp.where(last, pltpu.roll(got[1], back4, 1), pltpu.roll(got[0], back4, 1)),
        jnp.where(last, pltpu.roll(corner_down, back4, 1), pltpu.roll(got[1], back4, 1)),
    ]
    spot = slot & (SX - 1)
    for h in range(2):
        m, mine = got[h], packed[h]
        sides = jnp.where(
            (lane & 3) == 3,
            pltpu.roll(m, 1, 1) + pltpu.roll(mine, LANES - 1, 1),
            pltpu.roll(m, LANES - 1, 1) + pltpu.roll(mine, 1, 1),
        )
        over = jnp.where(sub == 0, m, pltpu.roll(m, 1, 0))
        under = jnp.where(sub == DEPTH - 1, m, pltpu.roll(m, DEPTH - 1, 0))
        diag = MASS_TERM + 3.0 * m + 0.5 * (ups[h] + downs[h] + sides + over + under)
        cut = jnp.where(spot == 7, m - downs[h], jnp.where(spot == 8, m - ups[h], 0.0))
        scale = RELAX_WEIGHT / diag
        scale_cut = RELAX_WEIGHT / (diag + 0.5 * cut)
        edge_m[h] = m
        for c in range(COMPS):
            edge_x[0, h, c] = scale * got[2 + 2 * c + h]
            edge_x[1, h, c] = scale_cut * got[2 + 2 * c + h]

    lane3 = lax.broadcasted_iota(jnp.int32, (SX, DEPTH, LANES), 2)
    plane3 = lax.broadcasted_iota(jnp.int32, (SX, DEPTH, LANES), 0)
    pair3 = ((lane3 + 1) & (LANES - 1)) >> 1
    pair = ((lane + 1) & (LANES - 1)) >> 1

    def shear_sides(s, _):
        base = s * SX
        mine = shear[pl.ds(base + 2, SX), 8:24, :]
        theirs = jnp.where(pair3 == 2 * ((plane3 + base) & 31), edge_m[s // 2][None], 0.0)
        both = jnp.concatenate([mine, theirs], axis=2).astype(BF16)
        moved = jnp.dot(both.reshape(SX * DEPTH, 2 * LANES), shift[...], preferred_element_type=F32)
        shear_lr[pl.ds(base + 1, SX)] = moved.reshape(SX, DEPTH, 2 * LANES)
        return 0

    lax.fori_loop(0, SUBS, shear_sides, 0)
    ends = jnp.concatenate(
        [
            jnp.concatenate([shear[1, 8:24, :], jnp.where(pair == 0, corner_up, 0.0)], axis=1),
            jnp.concatenate([shear[ROWS + 2, 8:24, :], jnp.where(pair == 0, corner_down, 0.0)], axis=1),
        ],
        axis=0,
    ).astype(BF16)
    moved = jnp.dot(ends, shift[...], preferred_element_type=F32)
    shear_lr[0] = moved[:DEPTH]
    shear_lr[ROWS + 1] = moved[DEPTH:]

    def first_sweep(p):
        m = shear[p + 1, 8:24, :]
        mu, md = shear[p, 8:24, :], shear[p + 2, 8:24, :]
        mo, mb = shear[p + 1, 7:23, :], shear[p + 1, 9:25, :]
        ml, mr = shear_lr[p, :, :LANES], shear_lr[p, :, LANES:]
        diag = MASS_TERM + 3.0 * m + 0.5 * ((mu + md) + (ml + mr) + (mo + mb))
        cut = 0.5 * jnp.where(lane == 7, m - mr, jnp.where(lane == 120, m - ml, 0.0))
        return m, mu, md, ml, mr, diag, cut

    for p, side, keep in ((0, 0, k_up), (ROWS + 1, 1, k_down)):
        _, _, _, _, _, diag, cut = first_sweep(p)
        b = rows_got[side, 2:5] * keep
        x0[:, p, 8:24, :] = (RELAX_WEIGHT / diag) * b
        x1[:, p, 8:24, :] = (RELAX_WEIGHT / (diag + cut)) * b

    def sweep_block(s, _):
        for q in range(SX):
            r = s * SX + q
            m, mu, md, ml, mr, diag, cut = first_sweep(r + 1)
            b = b_t[:, r]
            here = pair == 2 * (r & 31)
            gl[r] = m + ml
            gr[r] = m + mr
            theirs = jnp.where(here, edge_x[0, s // 2], 0.0).astype(BF16)
            for store, dg, xs, ls in ((s0, diag, x0, lhs0), (s1, diag + cut, x1, lhs1)):
                scale = RELAX_WEIGHT / dg
                store[r] = scale
                x = scale * b
                xs[:, r + 1, 8:24, :] = x
                ls[r, :, :, :LANES] = x.astype(BF16)
                ls[r, :, :, LANES:] = theirs
            if q in (7, 8):
                e = s * 2 + (q - 7)
                diag = diag + 0.5 * (m - (md if q == 7 else mu))
                theirs = jnp.where(here, edge_x[1, s // 2], 0.0).astype(BF16)
                for store, dg, xs, ls in ((sr0, diag, xr0, lhsr0), (sr1, diag + cut, xr1, lhsr1)):
                    scale = RELAX_WEIGHT / dg
                    store[e] = scale
                    x = scale * b
                    xs[:, e, 8:24, :] = x
                    ls[e, :, :, :LANES] = x.astype(BF16)
                    ls[e, :, :, LANES:] = theirs
        return 0

    lax.fori_loop(0, SUBS, sweep_block, 0)

    for o in range(1, nx):
        one(o, gx).wait_send()
        one(o, lax.rem(gx + nx - o, nx)).wait_recv()
    for o in range(1, ny):
        two(o, gy).start()

    block = 8

    def sides(i, _):
        for ls, ds in ((lhs0, lr0), (lhs1, lr1)):
            rows = ls[pl.ds(i * block, block)].reshape(block * COMPS * DEPTH, 2 * LANES)
            moved = jnp.dot(rows, shift[...], preferred_element_type=F32)
            ds[pl.ds(i * block, block)] = moved.reshape(block, COMPS, DEPTH, 2 * LANES)
        return 0

    lax.fori_loop(0, ROWS // block, sides, 0)
    for ls, ds in ((lhsr0, lrr0), (lhsr1, lrr1)):
        rows = ls[...].reshape(2 * SUBS * COMPS * DEPTH, 2 * LANES)
        moved = jnp.dot(rows, shift[...], preferred_element_type=F32)
        ds[...] = moved.reshape(2 * SUBS, COMPS, DEPTH, 2 * LANES)

    edge_lo, edge_hi = lane < 8, lane >= 120
    w0 = jnp.where(edge_lo | edge_hi, 0.25, 0.5).astype(F32)
    w1 = jnp.where(edge_lo, 0.25 * k_left, jnp.where(edge_hi, 0.25 * k_right, 0.0)).astype(F32)

    def second_block(s, _):
        for q in range(SX):
            r = s * SX + q
            m = shear[r + 2, 8:24, :]
            gu, gd = m + shear[r + 1, 8:24, :], m + shear[r + 3, 8:24, :]
            go, gb = m + shear[r + 2, 7:23, :], m + shear[r + 2, 9:25, :]
            g_l, g_r = gl[r], gr[r]
            if q < 8:
                keep = jnp.where((gx == 0) & (s == 0), 0.5, 1.0)
            else:
                keep = jnp.where((gx == nx - 1) & (s == SUBS - 1), 0.5, 1.0)
            b24 = b_t[:, r] * 2.4
            results = []
            for v, (ss, xs, lr, ssr, xsr, lrr) in enumerate(
                ((s0, x0, lr0, sr0, xr0, lrr0), (s1, x1, lr1, sr1, xr1, lrr1))
            ):
                hl = g_l if v == 0 else jnp.where(lane == 120, 0.0, g_l)
                hr = g_r if v == 0 else jnp.where(lane == 7, 0.0, g_r)
                scale = ss[r]
                above, below = xs[:, r, 8:24, :], xs[:, r + 2, 8:24, :]
                total = (b24 + gu * above + gd * below) + (
                    go * xs[:, r + 1, 7:23, :] + gb * xs[:, r + 1, 9:25, :]
                )
                total = total + (hl * lr[r, :, :, :LANES] + hr * lr[r, :, :, LANES:])
                x = scale * total
                if q in (6, 7, 8, 9):
                    e = s * 2 + (0 if q < 8 else 1)
                    if q == 6:
                        y = x + (scale * gd) * (xsr[:, e, 8:24, :] - below)
                    elif q == 9:
                        y = x + (scale * gu) * (xsr[:, e, 8:24, :] - above)
                    else:
                        other = gu * above if q == 7 else gd * below
                        y = (b24 + other) + (go * xsr[:, e, 7:23, :] + gb * xsr[:, e, 9:25, :])
                        y = y + (hl * lrr[e, :, :, :LANES] + hr * lrr[e, :, :, LANES:])
                        y = ssr[e] * y
                    x = 0.5 * x + (keep - 0.5) * y
                results.append(x)
            z0, z1 = results
            if q in (6, 7, 8, 9):
                loc_t[:, r] = w0 * z0 + w1 * z1
            else:
                loc_t[:, r] = (keep * w0) * z0 + (keep * w1) * z1
        return 0

    lax.fori_loop(0, SUBS, second_block, 0)
    for c in range(COMPS):
        for d in range(DEPTH):
            pltpu.make_async_copy(loc_t.at[c, :, d, :], loc_n.at[c, d], loc_sem).start()

    for o in range(1, ny):
        two(o, gy).wait_send()
        two(o, lax.rem(gy + ny - o, ny)).wait_recv()
    lane8 = lax.broadcasted_iota(jnp.int32, (KMAX, LANES), 1)
    sub8 = lax.broadcasted_iota(jnp.int32, (KMAX, LANES), 0)
    for s in range(SUBS):
        acc = jnp.zeros((KMAX, LANES), F32)
        for l in range(NLIST):
            n = table_ref[s, 0, l]
            row = coarse[(n & (ny - 1)) * nx + (n >> 6)]
            which = (n >> 4) & (SUBS - 1)
            row = jnp.where((lane1 >> 3) == which, row, 0.0)
            base = (s * NLIST + l) * KMAX
            acc = acc + gx_pieces[base : base + KMAX, :] * row
        answer = jnp.broadcast_to(jnp.sum(acc, axis=1, keepdims=True), (KMAX, LANES))
        answer = jnp.where(sub8 < tally_ref[s, 0], answer, 0.0)
        sol[s] = answer.astype(BF16).astype(F32)
    pltpu.make_async_copy(loc_n, loc_n, loc_sem).wait()

    def out_copy(s):
        part = pl.ds(s * SX, SX)
        return pltpu.make_async_copy(loc_n.at[:, :, part], out_hbm.at[:, :, part], out_sem.at[s])

    for s in range(SUBS):
        part = slice(s * SX, s * SX + SX)
        weights = [jnp.broadcast_to(sol[s, k : k + 1, :], (SX, LANES)) for k in range(KMAX)]

        def prolong(i, _):
            for j in range(4):
                d = i * 4 + j
                for c in range(COMPS):
                    total = loc_n[c, d, part, :]
                    for k in range(KMAX):
                        total = total + v_n[k, c, d, part, :].astype(F32) * weights[k]
                    loc_n[c, d, part, :] = total
            return 0

        lax.fori_loop(0, DEPTH // 4, prolong, 0)
        out_copy(s).start()
    for s in range(SUBS):
        out_copy(s).wait()


def local(
    equation_misfit,
    thermal_excess,
    spanning_vectors,
    global_solve_pieces,
    influencing_partition_table,
    spanning_vector_tally,
):
    nx, ny = lax.axis_size("gx"), lax.axis_size("gy")
    hbm = pl.BlockSpec(memory_space=pltpu.HBM)
    smem = pl.BlockSpec(memory_space=pltpu.SMEM)
    vmem = pl.BlockSpec(memory_space=pltpu.VMEM)
    plane = (DEPTH, LANES)
    wide = (DEPTH, 2 * LANES)
    cuts = 2 * SUBS

    def f32(*shape):
        return pltpu.VMEM(shape, F32)

    def low(*shape):
        return pltpu.VMEM(shape, BF16)

    dma = pltpu.SemaphoreType.DMA
    scratch = [
        f32(ROWS, *plane),
        f32(COMPS, ROWS, *plane),
        f32(COMPS, DEPTH, ROWS, LANES),
        low(KMAX, COMPS, DEPTH, ROWS, LANES),
        f32(ROWS + 4, 32, LANES),
        f32(ROWS + 2, *wide),
        f32(8, *plane),
        f32(2, 8, *plane),
        f32(2, 5, *plane),
        f32(2, 5, *plane),
        f32(4, *plane),
        f32(2, *plane),
        f32(2, 2, COMPS, *plane),
        low(2 * LANES, 2 * LANES),
        f32(COMPS, ROWS + 2, 32, LANES),
        f32(COMPS, ROWS + 2, 32, LANES),
        low(ROWS, COMPS, *wide),
        low(ROWS, COMPS, *wide),
        f32(ROWS, COMPS, *wide),
        f32(ROWS, COMPS, *wide),
        f32(ROWS, *plane),
        f32(ROWS, *plane),
        f32(ROWS, *plane),
        f32(ROWS, *plane),
        f32(COMPS, cuts, 32, LANES),
        f32(COMPS, cuts, 32, LANES),
        low(cuts, COMPS, *wide),
        low(cuts, COMPS, *wide),
        f32(cuts, COMPS, *wide),
        f32(cuts, COMPS, *wide),
        f32(cuts, *plane),
        f32(cuts, *plane),
        f32(COMPS, ROWS, *plane),
        f32(COMPS, DEPTH, ROWS, LANES),
        f32(SUBS * NLIST * KMAX, LANES),
        f32(nx * ny, 1, LANES),
        f32(SUBS, KMAX, LANES),
        dma,
        dma,
        dma,
        dma((2 * COMPS,)),
        dma,
        dma((SUBS,)),
        dma((8,)),
        dma((8,)),
        dma((nx - 1,)),
        dma((nx - 1,)),
        dma((ny - 1,)),
        dma((ny - 1,)),
    ]
    return pl.pallas_call(
        kernel,
        out_shape=jax.ShapeDtypeStruct(equation_misfit.shape, F32),
        in_specs=[hbm, hbm, hbm, vmem, smem, smem],
        out_specs=hbm,
        scratch_shapes=scratch,
        compiler_params=pltpu.CompilerParams(
            collective_id=0, has_side_effects=True, vmem_limit_bytes=56 * 2**20
        ),
        name="schwarz",
    )(
        equation_misfit,
        thermal_excess,
        spanning_vectors,
        global_solve_pieces,
        influencing_partition_table,
        spanning_vector_tally,
    )


def solution(mesh):
    return jax.shard_map(
        local,
        mesh=mesh,
        in_specs=(
            P(None, None, "gx", "gy"),
            P(None, "gx", "gy"),
            P(None, None, None, "gx", "gy"),
            P("gx", "gy", None, None, None),
            P("gx", "gy", None),
            P("gx", "gy"),
        ),
        out_specs=P(None, None, "gx", "gy"),
        check_vma=False,
    )
```

profile of v0, /device:TPU:1, one launch (start us, length us, event | category | flops | bytes accessed | tf_op | source)
XLA Modules:
  0.0 33.1 jit_solution(2359800633665012194)
XLA Ops:
  0.0 1.3 %copy.8.tally_ref = s32[4,1]{1,0:T(4,128)} copy(s32[4,1]{0,1:T(1,128)} %param.11) | data formatting | bytes 32 | tf_op args[5]
  1.3 1.8 %copy.7.g_ref = f32[4,1,9,8,8]{4,3,2,1,0:T(8,128)} copy(f32[4,1,9,8,8]{2,4,3,1,0:T(8,128)} %param.9) | data formatting | bytes 18432 | tf_op args[3]
  3.1 27.3 %schwarz.1 = f32[3,16,64,128]{3,2,1,0:T(8,128)} custom-call(f32[3,16,64,128]{3,2,1,0:T(8,128)} %b_hbm.1, f32[16,64,128]{2,1,0:T(8,128)} %te_hbm.1, bf16[8,3,16,64,128]{4,3,2,1,0:T(8,128)(2,1)} %v_hbm.1, f32[4,1,9,8,8]{4,3,2,1,0:T(8,128)} %copy.7.g_ref, s32[4,1,9]{2,1,0:T(1,128)} %table_ref.1, s32[4,1]{1,0:T(4,128)} %copy.8.tally_ref), custom_call_target="tpu_custom_call" | custom-call | tf_op jit(solution)/shard_map/schwarz/pallas_call | solution.py:591
  30.4 2.7 %copy.10 = f32[3,16,64,128]{3,2,1,0:T(8,128)} copy(f32[3,16,64,128]{3,2,1,0:T(8,128)} %schwarz.1) | data formatting | bytes 3145728
where the time goes:
time: 33.3 us; the launch traced here: 33.1 us
  Pallas kernels  27.3 us (82%)
  local copies, waits for them, and re-layouts  5.85 us (18%)
    pallas_call x1, Pallas kernels, local(): pl.pallas_call(kernel, out_shape=jax.ShapeDtypeStruct(equation_misfit.sha...  27.3 us
    unnamed x3, local copies, waits for them, and re-layouts  5.85 us

commit v1 on v0

v1 whole, which is shorter than its diff:
```python
import jax
import jax.numpy as jnp
from jax import lax
from jax.experimental import pallas as pl
from jax.experimental.pallas import tpu as pltpu
from jax.sharding import PartitionSpec as P

F32 = jnp.float32
BF16 = jnp.bfloat16
MESH = pl.DeviceIdType.MESH

COMPS = 3
DEPTH = 16
ROWS = 64
LANES = 128
SUBS = 4
SX = 16
KMAX = 8
NLIST = 9

MASS_TERM = 0.05
RELAX_WEIGHT = 0.8
ARRHENIUS_FACTOR = 6.0


def kernel(
    b_hbm,
    te_hbm,
    v_hbm,
    g_hbm,
    table_ref,
    tally_ref,
    loc_n,
    v_n,
    sol,
    te_t,
    b_t,
    b_n,
    pieces,
    shear,
    shear_lr,
    edge_own,
    edge_got,
    rows_own,
    rows_got,
    corner_got,
    edge_m,
    edge_x,
    edge_q,
    shift,
    x0,
    lhs,
    moved,
    s0,
    s1,
    q1,
    gl,
    gr,
    sr,
    qr,
    qr_lr,
    loc_t,
    sums,
    parts,
    coarse,
    te_sem,
    bt_sem,
    bn_sem,
    g_sem,
    v_sem,
    loc_sem,
    halo_send,
    halo_recv,
    one_send,
    one_recv,
    two_send,
    two_recv,
):
    gx = lax.axis_index("gx")
    gy = lax.axis_index("gy")
    nx = lax.axis_size("gx")
    ny = lax.axis_size("gy")
    up, down = lax.rem(gx + nx - 1, nx), lax.rem(gx + 1, nx)
    left, right = lax.rem(gy + ny - 1, ny), lax.rem(gy + 1, ny)

    for d in range(DEPTH):
        pltpu.make_async_copy(te_hbm.at[d], te_t.at[:, d, :], te_sem).start()
    for d in range(DEPTH):
        pltpu.make_async_copy(b_hbm.at[:, d], b_t.at[:, :, d, :], bt_sem).start()
    pltpu.make_async_copy(b_hbm, b_n, bn_sem).start()
    half = DEPTH // 2

    def v_copy(i):
        part = pl.ds((i % 2) * half, half)
        return pltpu.make_async_copy(
            v_hbm.at[:, i // 2, part], v_n.at[:, i // 2, part], v_sem.at[i]
        )

    for i in range(2 * COMPS):
        v_copy(i).start()
    for a in range(KMAX):
        pltpu.make_async_copy(g_hbm.at[:, 0, a], pieces.at[:, :, a, :], g_sem).start()

    barrier = pltpu.get_barrier_semaphore()
    for o in range(1, nx):
        pl.semaphore_signal(barrier, 1, device_id=(lax.rem(gx + o, nx), gy), device_id_type=MESH)
    for o in range(1, ny):
        pl.semaphore_signal(barrier, 1, device_id=(gx, lax.rem(gy + o, ny)), device_id_type=MESH)
    for px in (up, down):
        for py in (left, right):
            pl.semaphore_signal(barrier, 1, device_id=(px, py), device_id_type=MESH)

    lane = lax.broadcasted_iota(jnp.int32, (DEPTH, LANES), 1)
    sub = lax.broadcasted_iota(jnp.int32, (DEPTH, LANES), 0)

    wi = lax.broadcasted_iota(jnp.int32, (2 * LANES, 2 * LANES), 0)
    wj = lax.broadcasted_iota(jnp.int32, (2 * LANES, 2 * LANES), 1)
    own, to_left = wi < LANES, wj < LANES
    hit = (
        (own & to_left & (wi == wj - 1))
        | (own & ~to_left & (wi == wj - LANES + 1))
        | (~own & ((wi & 3) == 3) & (wj == 0))
        | (~own & ((wi & 3) == 0) & (wj == 2 * LANES - 1))
    )
    shift[...] = jnp.where(hit, 1.0, 0.0).astype(BF16)

    zeros = jnp.zeros((COMPS, 8, LANES), F32)
    zero = jnp.zeros((8, LANES), F32)

    def clear(p, _):
        x0[:, p, 0:8, :] = zeros
        x0[:, p, 24:32, :] = zeros
        q1[p, 0:8, :] = zero
        q1[p, 24:32, :] = zero
        return 0

    lax.fori_loop(0, ROWS + 2, clear, 0)

    def clear_cut(p, _):
        for v in range(2):
            qr[v, p, 0:8, :] = zero
            qr[v, p, 24:32, :] = zero
        return 0

    lax.fori_loop(0, 2 * SUBS, clear_cut, 0)
    sums[...] = jnp.zeros(sums.shape, F32)

    def put_shear(p, m):
        shear[p, 8:24, :] = m
        shear[p, 7:8, :] = m[0:1]
        shear[p, 24:25, :] = m[15:16]

    pltpu.make_async_copy(te_t, te_t, te_sem).wait()

    def make_shear(i, _):
        for j in range(4):
            r = i * 4 + j
            m = 1.0 / (1.0 + jnp.exp(ARRHENIUS_FACTOR * (1.0 - 1.0 / te_t[r])))
            put_shear(r + 2, m)
        return 0

    lax.fori_loop(0, ROWS // 4, make_shear, 0)
    pltpu.make_async_copy(b_t, b_t, bt_sem).wait()

    slot = ((lane + 2) & (LANES - 1)) >> 2

    def pack(i, held):
        for j in range(4):
            rr = i * 4 + j
            here = slot == rr
            new = []
            for f in range(4):
                for h in range(2):
                    r = rr + 32 * h
                    val = shear[r + 2, 8:24, :] if f == 0 else b_t[f - 1, r]
                    new.append(jnp.where(here, pltpu.roll(val, 4 * rr, 1), held[f * 2 + h]))
            held = tuple(new)
        return held

    packed = lax.fori_loop(0, 8, pack, tuple(jnp.zeros((DEPTH, LANES), F32) for _ in range(8)))
    for i in range(8):
        edge_own[i] = packed[i]
    for side, (near, next_) in enumerate(((0, 1), (ROWS - 1, ROWS - 2))):
        rows_own[side, 0] = shear[near + 2, 8:24, :]
        rows_own[side, 1] = shear[next_ + 2, 8:24, :]
        for c in range(COMPS):
            rows_own[side, 2 + c] = b_t[c, near]

    pl.semaphore_wait(barrier, (nx - 1) + (ny - 1) + 4)

    def halo(i, src, dst, px, py):
        return pltpu.make_async_remote_copy(
            src_ref=src,
            dst_ref=dst,
            send_sem=halo_send.at[i],
            recv_sem=halo_recv.at[i],
            device_id=(px, py),
            device_id_type=MESH,
        )

    halos = [
        halo(0, rows_own.at[0], rows_got.at[1], up, gy),
        halo(1, rows_own.at[1], rows_got.at[0], down, gy),
        halo(2, edge_own, edge_got.at[1], gx, left),
        halo(3, edge_own, edge_got.at[0], gx, right),
        halo(4, rows_own.at[0, 0], corner_got.at[3], up, left),
        halo(5, rows_own.at[0, 0], corner_got.at[2], up, right),
        halo(6, rows_own.at[1, 0], corner_got.at[1], down, left),
        halo(7, rows_own.at[1, 0], corner_got.at[0], down, right),
    ]
    for copy in halos:
        copy.start()

    pltpu.make_async_copy(b_n, b_n, bn_sem).wait()
    for i in range(2 * COMPS):
        v_copy(i).wait()

        def restrict(s, _):
            part = pl.ds(pl.multiple_of(s * SX, SX), SX)
            c = i // 2
            accs = [sums[s, k] for k in range(KMAX)]
            for j in range(half):
                d = (i % 2) * half + j
                low = b_n[c, d, part, :].astype(BF16).astype(F32)
                for k in range(KMAX):
                    accs[k] = accs[k] + v_n[k, c, d, part, :].astype(F32) * low
            for k in range(KMAX):
                sums[s, k] = accs[k]
            return 0

        lax.fori_loop(0, SUBS, restrict, 0)
    lane8 = lax.broadcasted_iota(jnp.int32, (KMAX, LANES), 1)
    sub8 = lax.broadcasted_iota(jnp.int32, (KMAX, LANES), 0)
    rhs = jnp.zeros((KMAX, LANES), F32)
    for s in range(SUBS):
        total = jnp.sum(jnp.sum(sums[s], axis=1), axis=1, keepdims=True)
        total = jnp.where(sub8 < tally_ref[0, s], total, 0.0)
        rhs = jnp.where(lane8 == gx * SUBS + s, total, rhs)
    parts[gx] = rhs

    def one(o, who):
        return pltpu.make_async_remote_copy(
            src_ref=parts.at[who],
            dst_ref=parts.at[who],
            send_sem=one_send.at[o - 1],
            recv_sem=one_recv.at[o - 1],
            device_id=(lax.rem(gx + o, nx), gy),
            device_id_type=MESH,
        )

    def two(o, who):
        return pltpu.make_async_remote_copy(
            src_ref=coarse.at[who],
            dst_ref=coarse.at[who],
            send_sem=two_send.at[o - 1],
            recv_sem=two_recv.at[o - 1],
            device_id=(gx, lax.rem(gy + o, ny)),
            device_id_type=MESH,
        )

    for o in range(1, nx):
        one(o, gx).start()

    for copy in halos:
        copy.wait()

    def flag(cond):
        return jnp.where(cond, 1.0, 0.0).astype(F32)

    k_up, k_down = flag(gx > 0), flag(gx < nx - 1)
    k_left, k_right = flag(gy > 0), flag(gy < ny - 1)
    put_shear(1, rows_got[0, 0] * k_up)
    put_shear(0, rows_got[0, 1] * k_up)
    put_shear(ROWS + 2, rows_got[1, 0] * k_down)
    put_shear(ROWS + 3, rows_got[1, 1] * k_down)
    from_left = (lane & 3) >= 2
    got = [
        jnp.where(from_left, edge_got[0, i] * k_left, edge_got[1, i] * k_right) for i in range(8)
    ]
    corner_up = jnp.where(
        lane == LANES - 1, corner_got[0] * (k_up * k_left), corner_got[1] * (k_up * k_right)
    )
    corner_down = jnp.where(
        lane == LANES - 1, corner_got[2] * (k_down * k_left), corner_got[3] * (k_down * k_right)
    )
    first, last = slot == 0, slot == 31
    back4 = LANES - 4
    ups = [
        jnp.where(first, corner_up, pltpu.roll(got[0], 4, 1)),
        jnp.where(first, pltpu.roll(got[0], 4, 1), pltpu.roll(got[1], 4, 1)),
    ]
    downs = [
        jnp.where(last, pltpu.roll(got[1], back4, 1), pltpu.roll(got[0], back4, 1)),
        jnp.where(last, pltpu.roll(corner_down, back4, 1), pltpu.roll(got[1], back4, 1)),
    ]
    spot = slot & (SX - 1)
    for h in range(2):
        m, mine = got[h], edge_own[h]
        sides = jnp.where(
            (lane & 3) == 3,
            pltpu.roll(m, 1, 1) + pltpu.roll(mine, LANES - 1, 1),
            pltpu.roll(m, LANES - 1, 1) + pltpu.roll(mine, 1, 1),
        )
        over = jnp.where(sub == 0, m, pltpu.roll(m, 1, 0))
        under = jnp.where(sub == DEPTH - 1, m, pltpu.roll(m, DEPTH - 1, 0))
        diag = MASS_TERM + 3.0 * m + 0.5 * (ups[h] + downs[h] + sides + over + under)
        cut = jnp.where(spot == 7, m - downs[h], jnp.where(spot == 8, m - ups[h], 0.0))
        scale = RELAX_WEIGHT / diag
        edge_m[h] = m
        edge_q[h] = diag / (diag + 0.5 * cut)
        for c in range(COMPS):
            edge_x[h, c] = scale * got[2 + 2 * c + h]

    lane3 = lax.broadcasted_iota(jnp.int32, (SX, DEPTH, LANES), 2)
    plane3 = lax.broadcasted_iota(jnp.int32, (SX, DEPTH, LANES), 0)
    pair3 = ((lane3 + 1) & (LANES - 1)) >> 1
    pair = ((lane + 1) & (LANES - 1)) >> 1

    def shear_sides(s, _):
        base = s * SX
        mine = shear[pl.ds(base + 2, SX), 8:24, :]
        theirs = jnp.where(pair3 == 2 * ((plane3 + base) & 31), edge_m[s // 2][None], 0.0)
        both = jnp.concatenate([mine, theirs], axis=2).astype(BF16)
        result = jnp.dot(both.reshape(SX * DEPTH, 2 * LANES), shift[...], preferred_element_type=F32)
        shear_lr[pl.ds(base + 1, SX)] = result.reshape(SX, DEPTH, 2 * LANES)
        return 0

    lax.fori_loop(0, SUBS, shear_sides, 0)
    ends = jnp.concatenate(
        [
            jnp.concatenate([shear[1, 8:24, :], jnp.where(pair == 0, corner_up, 0.0)], axis=1),
            jnp.concatenate([shear[ROWS + 2, 8:24, :], jnp.where(pair == 0, corner_down, 0.0)], axis=1),
        ],
        axis=0,
    ).astype(BF16)
    result = jnp.dot(ends, shift[...], preferred_element_type=F32)
    shear_lr[0] = result[:DEPTH]
    shear_lr[ROWS + 1] = result[DEPTH:]

    def first_sweep(p):
        m = shear[p + 1, 8:24, :]
        mu, md = shear[p, 8:24, :], shear[p + 2, 8:24, :]
        mo, mb = shear[p + 1, 7:23, :], shear[p + 1, 9:25, :]
        ml, mr = shear_lr[p, :, :LANES], shear_lr[p, :, LANES:]
        diag = MASS_TERM + 3.0 * m + 0.5 * ((mu + md) + (ml + mr) + (mo + mb))
        cut = 0.5 * jnp.where(lane == 7, m - mr, jnp.where(lane == 120, m - ml, 0.0))
        return m, mu, md, ml, mr, diag, cut

    ratio = 1.0 / RELAX_WEIGHT
    for p, side, keep in ((0, 0, k_up), (ROWS + 1, 1, k_down)):
        _, _, _, _, _, diag, cut = first_sweep(p)
        x0[:, p, 8:24, :] = (RELAX_WEIGHT / diag) * (rows_got[side, 2:5] * keep)
        q1[p, 8:24, :] = diag / (diag + cut)

    def sweep_block(s, _):
        for q in range(SX):
            r = s * SX + q
            m, mu, md, ml, mr, diag, cut = first_sweep(r + 1)
            gl[r] = m + ml
            gr[r] = m + mr
            scale = RELAX_WEIGHT / diag
            cut_scale = RELAX_WEIGHT / (diag + cut)
            ratio_diag = ratio * diag
            s0[r] = scale
            s1[r] = cut_scale
            q1[r + 1, 8:24, :] = cut_scale * ratio_diag
            x = scale * b_t[:, r]
            x0[:, r + 1, 8:24, :] = x
            here = pair == 2 * (r & 31)
            lhs[r, :, :, :LANES] = x.astype(BF16)
            lhs[r, :, :, LANES:] = jnp.where(here, edge_x[s // 2], 0.0).astype(BF16)
            if q in (7, 8):
                e = s * 2 + (q - 7)
                diag = diag + 0.5 * (m - (md if q == 7 else mu))
                for v, dg in ((0, diag), (1, diag + cut)):
                    scale = RELAX_WEIGHT / dg
                    sr[v, e] = scale
                    qr[v, e, 8:24, :] = scale * ratio_diag
        return 0

    lax.fori_loop(0, SUBS, sweep_block, 0)
    for v in range(2):
        rows = []
        for e in range(2 * SUBS):
            r = (e // 2) * SX + 7 + e % 2
            theirs = jnp.where(pair == 2 * (r & 31), edge_q[r // 32], 0.0)
            rows.append(jnp.concatenate([qr[v, e, 8:24, :], theirs], axis=1))
        rows = jnp.concatenate(rows, axis=0).astype(BF16)
        result = jnp.dot(rows, shift[...], preferred_element_type=F32)
        qr_lr[v] = result.reshape(2 * SUBS, DEPTH, 2 * LANES)

    edge_lo, edge_hi = lane < 8, lane >= 120
    w0 = jnp.where(edge_lo | edge_hi, 0.25, 0.5).astype(F32)
    w1 = jnp.where(edge_lo, 0.25 * k_left, jnp.where(edge_hi, 0.25 * k_right, 0.0)).astype(F32)
    few = 4

    def second_block(s, _):
        for j in range(SX // few):
            rows = lhs[pl.ds(s * SX + j * few, few)].reshape(few * COMPS * DEPTH, 2 * LANES)
            result = jnp.dot(rows, shift[...], preferred_element_type=F32)
            moved[j * few : (j + 1) * few] = result.reshape(few, COMPS, DEPTH, 2 * LANES)
        for q in range(SX):
            r = s * SX + q
            m = shear[r + 2, 8:24, :]
            gu, gd = m + shear[r + 1, 8:24, :], m + shear[r + 3, 8:24, :]
            go, gb = m + shear[r + 2, 7:23, :], m + shear[r + 2, 9:25, :]
            g_l, g_r = gl[r], gr[r]
            if q < 8:
                keep = jnp.where((gx == 0) & (s == 0), 0.5, 1.0)
            else:
                keep = jnp.where((gx == nx - 1) & (s == SUBS - 1), 0.5, 1.0)
            rest = keep - 0.5
            a0, a1 = w0 * s0[r], w1 * s1[r]
            qu, qd = q1[r, 8:24, :], q1[r + 2, 8:24, :]
            qo, qb = q1[r + 1, 7:23, :], q1[r + 1, 9:25, :]
            qm = q1[r + 1, 8:24, :]
            ql = jnp.where(lane == 121, pltpu.roll(qm, 1, 1), 1.0)
            ql = jnp.where(lane == 120, 0.0, ql)
            qn = jnp.where(lane == 6, pltpu.roll(qm, LANES - 1, 1), 1.0)
            qn = jnp.where(lane == 7, 0.0, qn)
            e = s * 2 + (0 if q < 8 else 1)
            if q in (7, 8):
                r0, r1 = rest * w0 * sr[0, e], rest * w1 * sr[1, e]
                a0, a1 = 0.5 * a0, 0.5 * a1
                ca = a0 + a1 + r0 + r1
                cu = (a0 + r0) + (a1 + r1) * qu if q == 7 else a0 + a1 * qu
                cd = (a0 + r0) + (a1 + r1) * qd if q == 8 else a0 + a1 * qd
                co = (a0 + a1 * qo) + (r0 * qr[0, e, 7:23, :] + r1 * qr[1, e, 7:23, :])
                cb = (a0 + a1 * qb) + (r0 * qr[0, e, 9:25, :] + r1 * qr[1, e, 9:25, :])
                r1l, r1r = jnp.where(lane == 120, 0.0, r1), jnp.where(lane == 7, 0.0, r1)
                cl = (a0 + a1 * ql) + (r0 * qr_lr[0, e, :, :LANES] + r1l * qr_lr[1, e, :, :LANES])
                cr = (a0 + a1 * qn) + (r0 * qr_lr[0, e, :, LANES:] + r1r * qr_lr[1, e, :, LANES:])
            else:
                if q in (6, 9):
                    k0 = 0.5 + rest * qr[0, e, 8:24, :]
                    near = a0 * k0
                    qx = qd if q == 6 else qu
                    near = near + a1 * (0.5 * qx + rest * qr[1, e, 8:24, :])
                a0, a1 = keep * a0, keep * a1
                ca = a0 + a1
                cu = near if q == 9 else a0 + a1 * qu
                cd = near if q == 6 else a0 + a1 * qd
                co = a0 + a1 * qo
                cb = a0 + a1 * qb
                cl = a0 + a1 * ql
                cr = a0 + a1 * qn
            ca = 2.4 * ca
            cu, cd, co, cb, cl, cr = cu * gu, cd * gd, co * go, cb * gb, cl * g_l, cr * g_r
            for c in range(COMPS):
                total = ca * b_t[c, r] + cu * x0[c, r, 8:24, :]
                total = total + (cd * x0[c, r + 2, 8:24, :] + co * x0[c, r + 1, 7:23, :])
                total = total + (cb * x0[c, r + 1, 9:25, :] + cl * moved[q, c, :, :LANES])
                loc_t[c, r] = total + cr * moved[q, c, :, LANES:]
        part = pl.ds(s * SX, SX)
        for d in range(DEPTH):
            pltpu.make_async_copy(
                loc_t.at[:, part, d, :], loc_n.at[:, d, part, :], loc_sem
            ).start()
        return 0

    lax.fori_loop(0, SUBS // 2, second_block, 0)

    for o in range(1, nx):
        one(o, gx).wait_send()
        one(o, lax.rem(gx + nx - o, nx)).wait_recv()
    joined = parts[0]
    for i in range(1, nx):
        joined = joined + parts[i]
    coarse[gy] = joined
    for o in range(1, ny):
        two(o, gy).start()
    lax.fori_loop(SUBS // 2, SUBS, second_block, 0)

    pltpu.make_async_copy(pieces, pieces, g_sem).wait()
    for o in range(1, ny):
        two(o, gy).wait_send()
        two(o, lax.rem(gy + ny - o, ny)).wait_recv()
    for s in range(SUBS):
        fetched = jnp.zeros((KMAX, LANES), F32)
        for l in range(NLIST):
            n = table_ref[s, 0, l]
            tile = jnp.where(lane8 == (n >> 4), coarse[n & (ny - 1)], 0.0)
            fetched = jnp.where(lane8 == l, jnp.sum(tile, axis=1, keepdims=True), fetched)
        acc = jnp.zeros((KMAX, NLIST), F32)
        for b in range(KMAX):
            acc = acc + pieces[s, b] * fetched[b : b + 1, :NLIST]
        answer = jnp.broadcast_to(jnp.sum(acc, axis=1, keepdims=True), (KMAX, LANES))
        answer = jnp.where(sub8 < tally_ref[0, s], answer, 0.0)
        sol[s] = answer.astype(BF16).astype(F32)
    pltpu.make_async_copy(loc_n, loc_n, loc_sem).wait()


def finish(loc_n, v_n, sol, out_hbm, out_v, out_sem):
    def out_copy(s):
        part = pl.ds(s * SX, SX)
        return pltpu.make_async_copy(out_v.at[:, :, part], out_hbm.at[:, :, part], out_sem.at[s])

    for s in range(SUBS):
        part = slice(s * SX, s * SX + SX)
        weights = [jnp.broadcast_to(sol[s, k : k + 1, :], (SX, LANES)) for k in range(KMAX)]

        def prolong(i, _):
            for j in range(4):
                d = i * 4 + j
                for c in range(COMPS):
                    total = loc_n[c, d, part, :]
                    for k in range(KMAX):
                        total = total + v_n[k, c, d, part, :].astype(F32) * weights[k]
                    out_v[c, d, part, :] = total
            return 0

        lax.fori_loop(0, DEPTH // 4, prolong, 0)
        out_copy(s).start()
    for s in range(SUBS):
        out_copy(s).wait()


def local(
    equation_misfit,
    thermal_excess,
    spanning_vectors,
    global_solve_pieces,
    influencing_partition_table,
    spanning_vector_tally,
):
    nx, ny = lax.axis_size("gx"), lax.axis_size("gy")
    hbm = pl.BlockSpec(memory_space=pltpu.HBM)
    smem = pl.BlockSpec(memory_space=pltpu.SMEM)
    vmem = pl.BlockSpec(memory_space=pltpu.VMEM)
    plane = (DEPTH, LANES)
    wide = (DEPTH, 2 * LANES)
    cuts = 2 * SUBS

    def f32(*shape):
        return pltpu.VMEM(shape, F32)

    def low(*shape):
        return pltpu.VMEM(shape, BF16)

    dma = pltpu.SemaphoreType.DMA
    scratch = [
        f32(ROWS, *plane),
        f32(COMPS, ROWS, *plane),
        f32(COMPS, DEPTH, ROWS, LANES),
        f32(SUBS, KMAX, KMAX, NLIST),
        f32(ROWS + 4, 32, LANES),
        f32(ROWS + 2, *wide),
        f32(8, *plane),
        f32(2, 8, *plane),
        f32(2, 5, *plane),
        f32(2, 5, *plane),
        f32(4, *plane),
        f32(2, *plane),
        f32(2, COMPS, *plane),
        f32(2, *plane),
        low(2 * LANES, 2 * LANES),
        f32(COMPS, ROWS + 2, 32, LANES),
        low(ROWS, COMPS, *wide),
        f32(SX, COMPS, *wide),
        f32(ROWS, *plane),
        f32(ROWS, *plane),
        f32(ROWS + 2, 32, LANES),
        f32(ROWS, *plane),
        f32(ROWS, *plane),
        f32(2, cuts, *plane),
        f32(2, cuts, 32, LANES),
        f32(2, cuts, *wide),
        f32(COMPS, ROWS, *plane),
        f32(SUBS, KMAX, SX, LANES),
        f32(nx, KMAX, LANES),
        f32(ny, KMAX, LANES),
        dma,
        dma,
        dma,
        dma,
        dma((2 * COMPS,)),
        dma,
        dma((8,)),
        dma((8,)),
        dma((nx - 1,)),
        dma((nx - 1,)),
        dma((ny - 1,)),
        dma((ny - 1,)),
    ]
    loc, vectors, sol = pl.pallas_call(
        kernel,
        out_shape=[
            pltpu.VMEM(equation_misfit.shape, F32),
            pltpu.VMEM(spanning_vectors.shape, BF16),
            pltpu.VMEM((SUBS, KMAX, LANES), F32),
        ],
        in_specs=[hbm, hbm, hbm, hbm, smem, smem],
        out_specs=[vmem] * 3,
        scratch_shapes=scratch,
        compiler_params=pltpu.CompilerParams(
            collective_id=0, has_side_effects=True, vmem_limit_bytes=52 * 2**20
        ),
        name="schwarz",
    )(
        equation_misfit,
        thermal_excess,
        spanning_vectors,
        jnp.transpose(global_solve_pieces, (0, 1, 3, 4, 2)),
        influencing_partition_table,
        jnp.transpose(spanning_vector_tally),
    )
    return pl.pallas_call(
        finish,
        out_shape=jax.ShapeDtypeStruct(equation_misfit.shape, F32),
        in_specs=[vmem] * 3,
        out_specs=hbm,
        scratch_shapes=[f32(COMPS, DEPTH, ROWS, LANES), dma((SUBS,))],
        compiler_params=pltpu.CompilerParams(vmem_limit_bytes=40 * 2**20),
        name="finish",
    )(loc, vectors, sol)


def solution(mesh):
    return jax.shard_map(
        local,
        mesh=mesh,
        in_specs=(
            P(None, None, "gx", "gy"),
            P(None, "gx", "gy"),
            P(None, None, None, "gx", "gy"),
            P("gx", "gy", None, None, None),
            P("gx", "gy", None),
            P("gx", "gy"),
        ),
        out_specs=P(None, None, "gx", "gy"),
        check_vma=False,
    )
```

time: 33.3 us -> 25.3 us (0.76)
  local copies, waits for them, and re-layouts: 5.85 us -> 0 us
  Pallas kernels: 27.3 us -> 25.1 us
    unnamed x3 -> x0, local copies, waits for them, and re-layouts: 5.85 us -> none
    pallas_call x1 -> x2, Pallas kernels: 27.3 us -> 25.1 us  [the longest x1 23 us: local(): pl.pallas_call(kernel, out_shape=[pltpu.VMEM(equation_misfit.shape, F32),...]
where the time goes in v1:
time: 25.3 us; the launch traced here: 25.2 us
  Pallas kernels  25.1 us (99%)
    pallas_call x1, Pallas kernels, local(): pl.pallas_call(kernel, out_shape=[pltpu.VMEM(equation_misfit.shape, F32),...  23 us
    pallas_call x1, Pallas kernels, local(): pl.pallas_call(finish, out_shape=jax.ShapeDtypeStruct(equation_misfit.sha...  2.13 us

profile of v1, /device:TPU:1, one launch (start us, length us, event | category | flops | bytes accessed | tf_op | source)
XLA Modules:
  0.0 25.2 jit_solution(4585318360614160628)
XLA Ops:
  0.0 23.0 %schwarz.1 = (f32[3,16,64,128]{3,2,1,0:T(8,128)S(1)}, bf16[8,3,16,64,128]{4,3,2,1,0:T(8,128)(2,1)S(1)}, f32[4,8,128]{2,1,0:T(8,128)S(1)}) custom-call(f32[3,16,64,128]{3,2,1,0:T(8,128)} %b_hbm.1, f32[16,64,128]{2,1,0:T(8,128)} %te_hbm.1, bf16[8,3,16,64,128]{4,3,2,1,0:T(8,128)(2,1)} %v_hbm.1, f32[4,1,8,8,9]{4,3,2,1,0:T(8,128)} %bitcast.2, ...), custom_call_target="tpu_custom_call" | custom-call | tf_op jit(solution)/shard_map/schwarz/pallas_call | solution.py:585
  23.0 2.1 %finish.1 = f32[3,16,64,128]{3,2,1,0:T(8,128)} custom-call(f32[3,16,64,128]{3,2,1,0:T(8,128)S(1)} %get-tuple-element.8.loc_n, bf16[8,3,16,64,128]{4,3,2,1,0:T(8,128)(2,1)S(1)} %get-tuple-element.9.v_n, f32[4,8,128]{2,1,0:T(8,128)S(1)} %get-tuple-element.10.sol), custom_call_target="tpu_custom_call" | custom-call | tf_op jit(solution)/shard_map/finish/pallas_call | solution.py:607

commit v2 on v1

--- a/solution.py
+++ b/solution.py
@@ -311,6 +311,15 @@
         for c in range(COMPS):
             edge_x[h, c] = scale * got[2 + 2 * c + h]
 
+    for o in range(1, nx):
+        one(o, gx).wait_send()
+        one(o, lax.rem(gx + nx - o, nx)).wait_recv()
+    joined = parts[0]
+    for i in range(1, nx):
+        joined = joined + parts[i]
+    coarse[gy] = joined
+    for o in range(1, ny):
+        two(o, gy).start()
     lane3 = lax.broadcasted_iota(jnp.int32, (SX, DEPTH, LANES), 2)
     plane3 = lax.broadcasted_iota(jnp.int32, (SX, DEPTH, LANES), 0)
     pair3 = ((lane3 + 1) & (LANES - 1)) >> 1
@@ -458,18 +467,8 @@
             ).start()
         return 0
 
-    lax.fori_loop(0, SUBS // 2, second_block, 0)
-
-    for o in range(1, nx):
-        one(o, gx).wait_send()
-        one(o, lax.rem(gx + nx - o, nx)).wait_recv()
-    joined = parts[0]
-    for i in range(1, nx):
-        joined = joined + parts[i]
-    coarse[gy] = joined
-    for o in range(1, ny):
-        two(o, gy).start()
-    lax.fori_loop(SUBS // 2, SUBS, second_block, 0)
+
+    lax.fori_loop(0, SUBS, second_block, 0)
 
     pltpu.make_async_copy(pieces, pieces, g_sem).wait()
     for o in range(1, ny):

time: 25.3 us -> 23.3 us (0.921)
  Pallas kernels: 25.1 us -> 23.1 us
    pallas_call x1, Pallas kernels: 23 us -> 21 us  [local(): pl.pallas_call(kernel, out_shape=[pltpu.VMEM(equation_misfit.shape, F32),...]
where the time goes in v2:
time: 23.3 us; the launch traced here: 23.1 us
  Pallas kernels  23.1 us (99%)
    pallas_call x1, Pallas kernels, local(): pl.pallas_call(kernel, out_shape=[pltpu.VMEM(equation_misfit.shape, F32),...  21 us
    pallas_call x1, Pallas kernels, local(): pl.pallas_call(finish, out_shape=jax.ShapeDtypeStruct(equation_misfit.sha...  2.13 us

profile of v2, /device:TPU:1, one launch (start us, length us, event | category | flops | bytes accessed | tf_op | source)
XLA Modules:
  0.0 23.1 jit_solution(7072244601733391479)
XLA Ops:
  0.0 21.0 %schwarz.1 = (f32[3,16,64,128]{3,2,1,0:T(8,128)S(1)}, bf16[8,3,16,64,128]{4,3,2,1,0:T(8,128)(2,1)S(1)}, f32[4,8,128]{2,1,0:T(8,128)S(1)}) custom-call(f32[3,16,64,128]{3,2,1,0:T(8,128)} %b_hbm.1, f32[16,64,128]{2,1,0:T(8,128)} %te_hbm.1, bf16[8,3,16,64,128]{4,3,2,1,0:T(8,128)(2,1)} %v_hbm.1, f32[4,1,8,8,9]{4,3,2,1,0:T(8,128)} %bitcast.2, ...), custom_call_target="tpu_custom_call" | custom-call | tf_op jit(solution)/shard_map/schwarz/pallas_call | solution.py:584
  21.0 2.1 %finish.1 = f32[3,16,64,128]{3,2,1,0:T(8,128)} custom-call(f32[3,16,64,128]{3,2,1,0:T(8,128)S(1)} %get-tuple-element.8.loc_n, bf16[8,3,16,64,128]{4,3,2,1,0:T(8,128)(2,1)S(1)} %get-tuple-element.9.v_n, f32[4,8,128]{2,1,0:T(8,128)S(1)} %get-tuple-element.10.sol), custom_call_target="tpu_custom_call" | custom-call | tf_op jit(solution)/shard_map/finish/pallas_call | solution.py:606

commit v3 on v2

--- a/solution.py
+++ b/solution.py
@@ -47,6 +47,8 @@
     edge_m,
     edge_x,
     edge_q,
+    edge_s,
+    end_s,
     shift,
     x0,
     lhs,
@@ -85,8 +87,6 @@
 
     for d in range(DEPTH):
         pltpu.make_async_copy(te_hbm.at[d], te_t.at[:, d, :], te_sem).start()
-    for d in range(DEPTH):
-        pltpu.make_async_copy(b_hbm.at[:, d], b_t.at[:, :, d, :], bt_sem).start()
     pltpu.make_async_copy(b_hbm, b_n, bn_sem).start()
     half = DEPTH // 2
 
@@ -98,6 +98,8 @@
 
     for i in range(2 * COMPS):
         v_copy(i).start()
+    for d in range(DEPTH):
+        pltpu.make_async_copy(b_hbm.at[:, d], b_t.at[:, :, d, :], bt_sem).start()
     for a in range(KMAX):
         pltpu.make_async_copy(g_hbm.at[:, 0, a], pieces.at[:, :, a, :], g_sem).start()
 
@@ -160,31 +162,32 @@
         return 0
 
     lax.fori_loop(0, ROWS // 4, make_shear, 0)
-    pltpu.make_async_copy(b_t, b_t, bt_sem).wait()
 
     slot = ((lane + 2) & (LANES - 1)) >> 2
 
-    def pack(i, held):
-        for j in range(4):
-            rr = i * 4 + j
-            here = slot == rr
-            new = []
-            for f in range(4):
-                for h in range(2):
-                    r = rr + 32 * h
-                    val = shear[r + 2, 8:24, :] if f == 0 else b_t[f - 1, r]
-                    new.append(jnp.where(here, pltpu.roll(val, 4 * rr, 1), held[f * 2 + h]))
-            held = tuple(new)
-        return held
-
-    packed = lax.fori_loop(0, 8, pack, tuple(jnp.zeros((DEPTH, LANES), F32) for _ in range(8)))
-    for i in range(8):
+    def pack(fields, step):
+        def some(i, held):
+            for j in range(step):
+                rr = i * step + j
+                here = slot == rr
+                new = []
+                for f in range(len(fields)):
+                    for h in range(2):
+                        val = fields[f](rr + 32 * h)
+                        new.append(jnp.where(here, pltpu.roll(val, 4 * rr, 1), held[f * 2 + h]))
+                held = tuple(new)
+            return held
+
+        blank = tuple(jnp.zeros((DEPTH, LANES), F32) for _ in range(2 * len(fields)))
+        return lax.fori_loop(0, 32 // step, some, blank)
+
+    packed = pack([lambda r: shear[r + 2, 8:24, :]], 8)
+    for i in range(2):
         edge_own[i] = packed[i]
-    for side, (near, next_) in enumerate(((0, 1), (ROWS - 1, ROWS - 2))):
+    borders = ((0, 1), (ROWS - 1, ROWS - 2))
+    for side, (near, next_) in enumerate(borders):
         rows_own[side, 0] = shear[near + 2, 8:24, :]
         rows_own[side, 1] = shear[next_ + 2, 8:24, :]
-        for c in range(COMPS):
-            rows_own[side, 2 + c] = b_t[c, near]
 
     pl.semaphore_wait(barrier, (nx - 1) + (ny - 1) + 4)
 
@@ -198,15 +201,22 @@
             device_id_type=MESH,
         )
 
+    shears, fields, ms, bs = pl.ds(0, 2), pl.ds(2, COMPS), pl.ds(0, 2), pl.ds(2, 2 * COMPS)
     halos = [
-        halo(0, rows_own.at[0], rows_got.at[1], up, gy),
-        halo(1, rows_own.at[1], rows_got.at[0], down, gy),
-        halo(2, edge_own, edge_got.at[1], gx, left),
-        halo(3, edge_own, edge_got.at[0], gx, right),
+        halo(0, rows_own.at[0, shears], rows_got.at[1, shears], up, gy),
+        halo(1, rows_own.at[1, shears], rows_got.at[0, shears], down, gy),
+        halo(2, edge_own.at[ms], edge_got.at[1, ms], gx, left),
+        halo(3, edge_own.at[ms], edge_got.at[0, ms], gx, right),
         halo(4, rows_own.at[0, 0], corner_got.at[3], up, left),
         halo(5, rows_own.at[0, 0], corner_got.at[2], up, right),
         halo(6, rows_own.at[1, 0], corner_got.at[1], down, left),
         halo(7, rows_own.at[1, 0], corner_got.at[0], down, right),
+    ]
+    halos_b = [
+        halo(8, rows_own.at[0, fields], rows_got.at[1, fields], up, gy),
+        halo(9, rows_own.at[1, fields], rows_got.at[0, fields], down, gy),
+        halo(10, edge_own.at[bs], edge_got.at[1, bs], gx, left),
+        halo(11, edge_own.at[bs], edge_got.at[0, bs], gx, right),
     ]
     for copy in halos:
         copy.start()
@@ -261,6 +271,15 @@
     for o in range(1, nx):
         one(o, gx).start()
 
+    pltpu.make_async_copy(b_t, b_t, bt_sem).wait()
+    packed = pack([lambda r, c=c: b_t[c, r] for c in range(COMPS)], 4)
+    for i in range(2 * COMPS):
+        edge_own[2 + i] = packed[i]
+    for side, (near, _) in enumerate(borders):
+        for c in range(COMPS):
+            rows_own[side, 2 + c] = b_t[c, near]
+    for copy in halos_b:
+        copy.start()
     for copy in halos:
         copy.wait()
 
@@ -274,9 +293,11 @@
     put_shear(ROWS + 2, rows_got[1, 0] * k_down)
     put_shear(ROWS + 3, rows_got[1, 1] * k_down)
     from_left = (lane & 3) >= 2
-    got = [
-        jnp.where(from_left, edge_got[0, i] * k_left, edge_got[1, i] * k_right) for i in range(8)
-    ]
+
+    def joined_edge(i):
+        return jnp.where(from_left, edge_got[0, i] * k_left, edge_got[1, i] * k_right)
+
+    got = [joined_edge(i) for i in range(2)]
     corner_up = jnp.where(
         lane == LANES - 1, corner_got[0] * (k_up * k_left), corner_got[1] * (k_up * k_right)
     )
@@ -305,21 +326,10 @@
         under = jnp.where(sub == DEPTH - 1, m, pltpu.roll(m, DEPTH - 1, 0))
         diag = MASS_TERM + 3.0 * m + 0.5 * (ups[h] + downs[h] + sides + over + under)
         cut = jnp.where(spot == 7, m - downs[h], jnp.where(spot == 8, m - ups[h], 0.0))
-        scale = RELAX_WEIGHT / diag
         edge_m[h] = m
         edge_q[h] = diag / (diag + 0.5 * cut)
-        for c in range(COMPS):
-            edge_x[h, c] = scale * got[2 + 2 * c + h]
-
-    for o in range(1, nx):
-        one(o, gx).wait_send()
-        one(o, lax.rem(gx + nx - o, nx)).wait_recv()
-    joined = parts[0]
-    for i in range(1, nx):
-        joined = joined + parts[i]
-    coarse[gy] = joined
-    for o in range(1, ny):
-        two(o, gy).start()
+        edge_s[h] = RELAX_WEIGHT / diag
+
     lane3 = lax.broadcasted_iota(jnp.int32, (SX, DEPTH, LANES), 2)
     plane3 = lax.broadcasted_iota(jnp.int32, (SX, DEPTH, LANES), 0)
     pair3 = ((lane3 + 1) & (LANES - 1)) >> 1
@@ -346,6 +356,15 @@
     shear_lr[0] = result[:DEPTH]
     shear_lr[ROWS + 1] = result[DEPTH:]
 
+    for o in range(1, nx):
+        one(o, gx).wait_send()
+        one(o, lax.rem(gx + nx - o, nx)).wait_recv()
+    joined = parts[0]
+    for i in range(1, nx):
+        joined = joined + parts[i]
+    coarse[gy] = joined
+    for o in range(1, ny):
+        two(o, gy).start()
     def first_sweep(p):
         m = shear[p + 1, 8:24, :]
         mu, md = shear[p, 8:24, :], shear[p + 2, 8:24, :]
@@ -356,9 +375,9 @@
         return m, mu, md, ml, mr, diag, cut
 
     ratio = 1.0 / RELAX_WEIGHT
-    for p, side, keep in ((0, 0, k_up), (ROWS + 1, 1, k_down)):
+    for p, side in ((0, 0), (ROWS + 1, 1)):
         _, _, _, _, _, diag, cut = first_sweep(p)
-        x0[:, p, 8:24, :] = (RELAX_WEIGHT / diag) * (rows_got[side, 2:5] * keep)
+        end_s[side] = RELAX_WEIGHT / diag
         q1[p, 8:24, :] = diag / (diag + cut)
 
     def sweep_block(s, _):
@@ -375,9 +394,7 @@
             q1[r + 1, 8:24, :] = cut_scale * ratio_diag
             x = scale * b_t[:, r]
             x0[:, r + 1, 8:24, :] = x
-            here = pair == 2 * (r & 31)
             lhs[r, :, :, :LANES] = x.astype(BF16)
-            lhs[r, :, :, LANES:] = jnp.where(here, edge_x[s // 2], 0.0).astype(BF16)
             if q in (7, 8):
                 e = s * 2 + (q - 7)
                 diag = diag + 0.5 * (m - (md if q == 7 else mu))
@@ -397,6 +414,23 @@
         rows = jnp.concatenate(rows, axis=0).astype(BF16)
         result = jnp.dot(rows, shift[...], preferred_element_type=F32)
         qr_lr[v] = result.reshape(2 * SUBS, DEPTH, 2 * LANES)
+
+    for copy in halos_b:
+        copy.wait()
+    for side, p, keep in ((0, 0, k_up), (1, ROWS + 1, k_down)):
+        x0[:, p, 8:24, :] = end_s[side] * (rows_got[side, 2:5] * keep)
+    for h in range(2):
+        for c in range(COMPS):
+            edge_x[h, c] = edge_s[h] * joined_edge(2 + 2 * c + h)
+
+    def sweep_edges(i, _):
+        for j in range(8):
+            r = i * 8 + j
+            here = pair == 2 * (r & 31)
+            lhs[r, :, :, LANES:] = jnp.where(here, edge_x[i // 4], 0.0).astype(BF16)
+        return 0
+
+    lax.fori_loop(0, ROWS // 8, sweep_edges, 0)
 
     edge_lo, edge_hi = lane < 8, lane >= 120
     w0 = jnp.where(edge_lo | edge_hi, 0.25, 0.5).astype(F32)
@@ -552,6 +586,8 @@
         f32(2, *plane),
         f32(2, COMPS, *plane),
         f32(2, *plane),
+        f32(2, *plane),
+        f32(2, *plane),
         low(2 * LANES, 2 * LANES),
         f32(COMPS, ROWS + 2, 32, LANES),
         low(ROWS, COMPS, *wide),
@@ -574,8 +610,8 @@
         dma,
         dma((2 * COMPS,)),
         dma,
-        dma((8,)),
-        dma((8,)),
+        dma((12,)),
+        dma((12,)),
         dma((nx - 1,)),
         dma((nx - 1,)),
         dma((ny - 1,)),

time: 23.3 us -> 22.9 us (0.983)
  Pallas kernels: 23.1 us -> 22.8 us
    pallas_call x1, Pallas kernels: 21 us -> 20.6 us  [local(): pl.pallas_call(kernel, out_shape=[pltpu.VMEM(equation_misfit.shape, F32),...]
where the time goes in v3:
time: 22.9 us; the launch traced here: 22.8 us
  Pallas kernels  22.8 us (100%)
    pallas_call x1, Pallas kernels, local(): pl.pallas_call(kernel, out_shape=[pltpu.VMEM(equation_misfit.shape, F32),...  20.6 us
    pallas_call x1, Pallas kernels, local(): pl.pallas_call(finish, out_shape=jax.ShapeDtypeStruct(equation_misfit.sha...  2.13 us

profile of v3, /device:TPU:1, one launch (start us, length us, event | category | flops | bytes accessed | tf_op | source)
XLA Modules:
  0.0 22.8 jit_solution(5601933628948091863)
XLA Ops:
  0.0 20.6 %schwarz.1 = (f32[3,16,64,128]{3,2,1,0:T(8,128)S(1)}, bf16[8,3,16,64,128]{4,3,2,1,0:T(8,128)(2,1)S(1)}, f32[4,8,128]{2,1,0:T(8,128)S(1)}) custom-call(f32[3,16,64,128]{3,2,1,0:T(8,128)} %b_hbm.1, f32[16,64,128]{2,1,0:T(8,128)} %te_hbm.1, bf16[8,3,16,64,128]{4,3,2,1,0:T(8,128)(2,1)} %v_hbm.1, f32[4,1,8,8,9]{4,3,2,1,0:T(8,128)} %bitcast.2, ...), custom_call_target="tpu_custom_call" | custom-call | tf_op jit(solution)/shard_map/schwarz/pallas_call | solution.py:620
  20.6 2.1 %finish.1 = f32[3,16,64,128]{3,2,1,0:T(8,128)} custom-call(f32[3,16,64,128]{3,2,1,0:T(8,128)S(1)} %get-tuple-element.8.loc_n, bf16[8,3,16,64,128]{4,3,2,1,0:T(8,128)(2,1)S(1)} %get-tuple-element.9.v_n, f32[4,8,128]{2,1,0:T(8,128)S(1)} %get-tuple-element.10.sol), custom_call_target="tpu_custom_call" | custom-call | tf_op jit(solution)/shard_map/finish/pallas_call | solution.py:642
